TPU v7x, 256 devices: a whole 4x4x8 slice. The times are simulated.
256 devices in a mesh: slab: 4 (over x), xs: 64 (over z, y, core).
Axes of the slice: x: 4, y: 4, z: 8, core: 2. Of those that a mesh axis runs over, the one named last changes fastest.
Arguments:
- perturbation: int32 [4, 1024, 1024], P('slab', 'xs'), may hold values from 0 to 15
- seeds: int32 [4, 32, 2], P('slab'), may hold values from 1 to 8, as said below
Outputs:
- modes: float32 [4, 32, 1024, 1024], P('slab', None, 'xs')
- projected: float32 [4, 32, 32], P('slab')
- correlations: float32 [4, 32, 32], P('slab')
Inputs may be any that keep to these rules, and one draw needn't show every extreme that they name: `seeds`: within one slice the 32 pairs (first, second) are distinct; the pairs (1, 1) and (8, 8) occur in every slice.
All inputs are finite; a program needn't handle non-finite values.
Results may differ from a plain program's by a relative error of at most 0.0003.
Values sent between devices are 32-bit elements; how exact they have to be, the bound alone decides.
No kernel may reach another device: no remote copies, remote signals or barrier semaphores. Data moves between devices by JAX's collectives and lax.ppermute only.
A program may use at most 64 MiB of HBM per device.

v0:
```python
import math
import jax
import jax.numpy as jnp
from jax import lax
from jax.sharding import PartitionSpec as P

NX = 1024
SWEEPS = 4


def padded_2(array, sides, width):
    for axis, dim in sides:
        size, length = (lax.axis_size(axis), array.shape[dim])
        up = [(i, (i + 1) % size) for i in range(size - 1)]
        down = [(j, i) for i, j in up]
        last = lax.slice_in_dim(array, length - width, length, axis=dim)
        first = lax.slice_in_dim(array, 0, width, axis=dim)
        before = lax.ppermute(last, axis, up)
        after = lax.ppermute(first, axis, down)
        array = jnp.concatenate([before, array, after], axis=dim)
    return array


def from_behind(block, axis, distance):
    devices = range(lax.axis_size(axis))
    route = [(i - distance, i) for i in devices if i - distance in devices]
    return lax.ppermute(block, axis, route)


def potential(pert, row_ids, width):
    xpos = (row_ids.astype(jnp.float32)[:, None] + 0.5) / NX - 0.5
    ypos = (jnp.arange(width).astype(jnp.float32)[None, :] + 0.5) / width - 0.5
    conf = 4.0 * (xpos * xpos + 0.6 * ypos * ypos + 0.5 * xpos)
    return conf[None] + 0.1 * pert.astype(jnp.float32)


def start_basis(seeds_f, row_ids, width):
    scale = 2.0 / math.sqrt((NX + 1) * (width + 1))
    rows_f = row_ids.astype(jnp.float32) + 1.0
    cols_f = jnp.arange(width).astype(jnp.float32) + 1.0
    along_x = jnp.sin(math.pi * seeds_f[:, :, 0:1] * rows_f[None, None, :] / (NX + 1))
    along_y = jnp.sin(math.pi * seeds_f[:, :, 1:2] * cols_f[None, None, :] / (width + 1))
    return scale * along_x[:, :, :, None] * along_y[:, :, None, :]


def apply_ham(basis, pot):
    padded = padded_2(basis, (("xs", 2),), 1)
    sided = jnp.pad(basis, ((0, 0), (0, 0), (0, 0), (1, 1)))
    beside = padded[:, :, 2:, :] + padded[:, :, :-2, :] + sided[:, :, :, 2:] + sided[:, :, :, :-2]
    return 4.0 * basis - beside + pot[:, None] * basis


def orthonormal(trial, gram):
    lower = jnp.linalg.cholesky(gram)
    identity = jnp.broadcast_to(jnp.eye(gram.shape[1], dtype=gram.dtype), gram.shape)
    inverse = lax.linalg.triangular_solve(lower, identity, left_side=True, lower=True)
    return jnp.einsum("skij,smk->smij", trial, inverse, precision=lax.Precision.HIGHEST)


def local(perturbation, seeds):
    rows = perturbation.shape[1]
    width = perturbation.shape[2]
    row_ids = lax.axis_index("xs") * rows + jnp.arange(rows)
    pot = potential(perturbation, row_ids, width)
    seeds_f = seeds.astype(jnp.float32)
    basis = start_basis(seeds_f, row_ids, width)
    for sweep in range(SWEEPS):
        trial = 13.0 * basis - apply_ham(basis, pot)
        part_gram = jnp.einsum("mij,nij->mn", trial[0], trial[0], precision=lax.Precision.HIGHEST)
        pieces = [lax.psum(part_gram, "xs")]
        gram = jnp.stack(pieces, axis=0)
        basis = orthonormal(trial, gram)
    image = apply_ham(basis, pot)
    ham_part = jnp.einsum("smij,snij->smn", basis, image, precision=lax.Precision.HIGHEST)
    next_basis = from_behind(basis[0], "slab", -1)
    following = jnp.concatenate([basis[1:], next_basis[None]], axis=0)
    over_part = jnp.einsum("smij,snij->smn", basis, following, precision=lax.Precision.HIGHEST)
    projected, correlations = lax.psum((ham_part, over_part), "xs")
    modes = basis * math.sqrt(NX * width)
    return (modes, projected, correlations)


def solution(mesh):
    placed = (P("slab", "xs", None), P("slab", None, None))
    return jax.shard_map(
        local,
        mesh=mesh,
        in_specs=placed,
        out_specs=(P("slab", None, "xs", None), P("slab", None, None), P("slab", None, None)),
        check_vma=False,
    )
```

profile of v0, /device:TPU:132, one launch (start us, length us, event | category | flops | bytes accessed | tf_op | source)
XLA Modules:
  0.0 1377.9 jit_solution(3904637582738356508)
XLA Ops:
  2.2 3.9 collective-permute-start
  6.1 1.9 collective-permute-start.1
  8.6 7.1 collective-permute-done.1
  18.9 246.2 %psum.42 = f32[1,32,32]{1,2,0:T(8,128)S(1)} all-reduce(f32[1,32,32]{1,2,0:T(8,128)S(1)} %convolution_bitcast_fusion.8), channel_id=1, replica_groups=mesh['slab'=4,'xs'=64] {'xs'}, use_global_device_ids=true, to_apply=%region_0.1 | all-reduce | flops 1024 | bytes 8192 | tf_op jit(solution)/shard_map/psum | solution.py:70
  265.2 2.9 custom-call.12
  269.4 2.4 custom-call.13
  274.0 1.9 collective-permute-start.2
  276.0 2.4 collective-permute-start.3
  278.5 7.1 collective-permute-done.3
  288.5 246.4 %psum.43 = f32[1,32,32]{1,2,0:T(8,128)S(1)} all-reduce(f32[1,32,32]{1,2,0:T(8,128)S(1)} %convolution_bitcast_fusion.6), channel_id=1, replica_groups=mesh['slab'=4,'xs'=64] {'xs'}, use_global_device_ids=true, to_apply=%region_3.0 | all-reduce | flops 1024 | bytes 8192 | tf_op jit(solution)/shard_map/psum | solution.py:70
  535.0 2.9 custom-call.14
  539.2 2.4 custom-call.15
  543.8 1.9 collective-permute-start.4
  545.8 2.4 collective-permute-start.5
  548.3 7.1 collective-permute-done.5
  558.3 246.2 %psum.44 = f32[1,32,32]{1,2,0:T(8,128)S(1)} all-reduce(f32[1,32,32]{1,2,0:T(8,128)S(1)} %convolution_bitcast_fusion.4), channel_id=1, replica_groups=mesh['slab'=4,'xs'=64] {'xs'}, use_global_device_ids=true, to_apply=%region_4.0 | all-reduce | flops 1024 | bytes 8192 | tf_op jit(solution)/shard_map/psum | solution.py:70
  804.6 2.9 custom-call.16
  808.9 2.4 custom-call.17
  813.5 1.9 collective-permute-start.6
  815.4 2.6 collective-permute-start.7
  818.0 7.0 collective-permute-done.7
  827.9 246.2 %psum.45 = f32[1,32,32]{1,2,0:T(8,128)S(1)} all-reduce(f32[1,32,32]{1,2,0:T(8,128)S(1)} %convolution_bitcast_fusion.2), channel_id=1, replica_groups=mesh['slab'=4,'xs'=64] {'xs'}, use_global_device_ids=true, to_apply=%region_5.0 | all-reduce | flops 1024 | bytes 8192 | tf_op jit(solution)/shard_map/psum | solution.py:70
  1074.2 2.9 custom-call.18
  1078.5 2.4 custom-call.19
  1083.0 2.4 collective-permute-start.10
  1085.5 1.9 collective-permute-start.8
  1087.4 2.7 collective-permute-start.9
  1090.3 2.5 copy.13
  1092.8 4.2 collective-permute-done.9
  1097.0 2.5 fusion.43
  1099.6 27.7 %collective-permute-done.10 = f32[32,16,1024]{2,0,1:T(8,128)S(1)} collective-permute-done((f32[32,16,1024]{2,0,1:T(8,128)S(1)}, f32[32,16,1024]{2,0,1:T(8,128)S(1)}, u32[]{:S(2)}, u32[]{:S(2)}) %collective-permute-start.10) | collective-permute-done | bytes 2097184 | tf_op jit(solution)/shard_map/ppermute | solution.py:27
  1129.1 248.7 %all-reduce.5 = (f32[1,32,32]{2,1,0:T(8,128)}, f32[1,32,32]{2,1,0:T(8,128)}) all-reduce(f32[1,32,32]{2,1,0:T(8,128)S(1)} %fusion.43, f32[1,32,32]{2,1,0:T(8,128)S(1)} %convolution_bitcast_fusion), channel_id=1, replica_groups=mesh['slab'=4,'xs'=64] {'xs'}, use_global_device_ids=true, to_apply=%region_6.9 | all-reduce | flops 2048 | bytes 16384 | tf_op jit(solution)/shard_map/psum | solution.py:78
  (60 shorter events, 30.4 us)
Async XLA Ops:
  0.6 7.5 copy-start
  2.2 6.4 collective-permute-start
  6.1 9.6 collective-permute-start.1
  274.0 4.4 collective-permute-start.2
  276.0 9.6 collective-permute-start.3
  543.8 4.4 collective-permute-start.4
  545.8 9.6 collective-permute-start.5
  813.5 4.6 collective-permute-start.6
  815.4 9.6 collective-permute-start.7
  1083.0 44.3 %collective-permute-start.10 = (f32[32,16,1024]{2,0,1:T(8,128)S(1)}, f32[32,16,1024]{2,0,1:T(8,128)S(1)}, u32[]{:S(2)}, u32[]{:S(2)}) collective-permute-start(f32[32,16,1024]{2,0,1:T(8,128)S(1)} %fusion.86), channel_id=1, source_target_pairs={{64,0},{128,64},{192,128},{65,1},{129,65},{193,129},{66,2},{130,66... | collective-permute-start | bytes 6291464 | tf_op jit(solution)/shard_map/ppermute | solution.py:27
  1085.5 7.3 collective-permute-start.8
  1087.4 9.6 collective-permute-start.9
where the time goes:
time: 1380 us
  blocking collectives  1230 us (89%)
  waiting for transfers between devices  60.8 us (4%)
  other arithmetic  33.4 us (2%)
  starting transfers between devices  26.1 us (2%)
  matrix products  19.9 us (1%)
    psum x4, blocking collectives, local(): pieces = [lax.psum(part_gram, 'xs')]  985 us
    psum x1, blocking collectives, local(): projected, correlations = lax.psum((ham_part, over_part), 'xs')  249 us
    ppermute x5, waiting for transfers between devices, padded_2(): before = lax.ppermute(last, axis, up)  32.5 us
    ppermute x1, waiting for transfers between devices, from_behind(): return lax.ppermute(block, axis, route)  27.7 us
  transfers between devices with their start and end apart: 11, of which 9 were waited for; matrix products, arithmetic and copies ran while one was open for 0% of the time, Pallas kernels for 0%

commit v1 on v0

--- a/solution.py
+++ b/solution.py
@@ -67,7 +67,7 @@
     for sweep in range(SWEEPS):
         trial = 13.0 * basis - apply_ham(basis, pot)
         part_gram = jnp.einsum("mij,nij->mn", trial[0], trial[0], precision=lax.Precision.HIGHEST)
-        pieces = [lax.psum(part_gram, "xs")]
+        pieces = [jnp.sum(lax.all_gather(part_gram, "xs"), axis=0)]
         gram = jnp.stack(pieces, axis=0)
         basis = orthonormal(trial, gram)
     image = apply_ham(basis, pot)

time: 1380 us -> 608 us (0.44)
  blocking collectives: 1230 us -> 439 us
    psum x4 -> x0, blocking collectives: 985 us -> none  [local(): pieces = [lax.psum(part_gram, 'xs')]]
    all_gather x0 -> x4, blocking collectives: none -> 191 us  [local(): pieces = [jnp.sum(lax.all_gather(part_gram, 'xs'), axis=0)]]
  transfers between devices with their start and end apart: 11 -> 11, of which waited for: 9 -> 10; matrix products, arithmetic and copies ran while one was open for 0% -> 1% of each run, Pallas kernels for 0% -> 0%
where the time goes in v1:
time: 608 us; the launch traced here: 598 us
  blocking collectives  439 us (72%)
  waiting for transfers between devices  66 us (11%)
  starting transfers between devices  34.3 us (6%)
  other arithmetic  33.9 us (6%)
  matrix products  19.9 us (3%)
    psum x1, blocking collectives, local(): projected, correlations = lax.psum((ham_part, over_part), 'xs')  249 us
    all_gather x4, blocking collectives, local(): pieces = [jnp.sum(lax.all_gather(part_gram, 'xs'), axis=0)]  191 us
    ppermute x5, waiting for transfers between devices, padded_2(): before = lax.ppermute(last, axis, up)  33.4 us
    ppermute x1, waiting for transfers between devices, from_behind(): return lax.ppermute(block, axis, route)  30.9 us
    ppermute x5, starting transfers between devices, padded_2(): after = lax.ppermute(first, axis, down)  21.8 us
    another operation x12, other arithmetic, orthonormal(): lower = jnp.linalg.cholesky(gram)  14.4 us
    another operation x8, other arithmetic, orthonormal(): lax.linalg.triangular_solve(lower, identity, left_side=True, lower=True)  12.3 us
  transfers between devices with their start and end apart: 11, of which 10 were waited for; matrix products, arithmetic and copies ran while one was open for 1% of the time, Pallas kernels for 0%

profile of v1, /device:TPU:132, one launch (start us, length us, event | category | flops | bytes accessed | tf_op | source)
XLA Modules:
  0.0 597.8 jit_solution(7790661959720557487)
XLA Ops:
  2.2 3.9 collective-permute-start
  6.1 1.9 collective-permute-start.1
  8.6 7.1 %collective-permute-done.1 = f32[1,32,1,1024]{3,1,2,0:T(8,128)S(1)} collective-permute-done((f32[1,32,1,1024]{3,1,2,0:T(8,128)S(1)}, f32[1,32,1,1024]{3,1,2,0:T(8,128)S(1)}, u32[]{:S(2)}, u32[]{:S(2)}) %collective-permute-start.1) | collective-permute-done | bytes 131104 | tf_op jit(solution)/shard_map/ppermute | solution.py:18
  18.9 47.8 %all-gather = f32[2048,32]{1,0:T(8,128)S(1)} all-gather(f32[32,32]{1,0:T(8,128)S(1)} %convolution_bitcast_fusion.8), channel_id=2, replica_groups=mesh['slab'=4,'xs'=64] {'xs'}, dimensions={0}, use_global_device_ids=true | all-gather | bytes 266240 | tf_op jit(solution)/shard_map/all_gather | solution.py:70
  67.0 2.9 custom-call.12
  71.3 2.4 custom-call.13
  75.9 4.6 collective-permute-start.2
  80.4 2.4 collective-permute-start.3
  82.9 7.1 %collective-permute-done.3 = f32[1,32,1,1024]{3,1,2,0:T(8,128)S(1)} collective-permute-done((f32[1,32,1,1024]{3,1,2,0:T(8,128)S(1)}, f32[1,32,1,1024]{3,1,2,0:T(8,128)S(1)}, u32[]{:S(2)}, u32[]{:S(2)}) %collective-permute-start.3) | collective-permute-done | bytes 131104 | tf_op jit(solution)/shard_map/ppermute | solution.py:18
  93.0 47.2 %all-gather.1 = f32[2048,32]{1,0:T(8,128)S(1)} all-gather(f32[32,32]{1,0:T(8,128)S(1)} %convolution_bitcast_fusion.6), channel_id=3, replica_groups=mesh['slab'=4,'xs'=64] {'xs'}, dimensions={0}, use_global_device_ids=true | all-gather | bytes 266240 | tf_op jit(solution)/shard_map/all_gather | solution.py:70
  140.5 2.9 custom-call.14
  144.8 2.4 custom-call.15
  149.4 4.5 collective-permute-start.4
  153.9 1.9 collective-permute-start.5
  156.4 7.1 %collective-permute-done.5 = f32[1,32,1,1024]{3,1,2,0:T(8,128)S(1)} collective-permute-done((f32[1,32,1,1024]{3,1,2,0:T(8,128)S(1)}, f32[1,32,1,1024]{3,1,2,0:T(8,128)S(1)}, u32[]{:S(2)}, u32[]{:S(2)}) %collective-permute-start.5) | collective-permute-done | bytes 131104 | tf_op jit(solution)/shard_map/ppermute | solution.py:18
  166.5 48.0 %all-gather.2 = f32[2048,32]{1,0:T(8,128)S(1)} all-gather(f32[32,32]{1,0:T(8,128)S(1)} %convolution_bitcast_fusion.4), channel_id=4, replica_groups=mesh['slab'=4,'xs'=64] {'xs'}, dimensions={0}, use_global_device_ids=true | all-gather | bytes 266240 | tf_op jit(solution)/shard_map/all_gather | solution.py:70
  214.8 2.9 custom-call.16
  219.1 2.4 custom-call.17
  223.7 4.5 collective-permute-start.6
  228.2 1.9 collective-permute-start.7
  230.7 7.1 %collective-permute-done.7 = f32[1,32,1,1024]{3,1,2,0:T(8,128)S(1)} collective-permute-done((f32[1,32,1,1024]{3,1,2,0:T(8,128)S(1)}, f32[1,32,1,1024]{3,1,2,0:T(8,128)S(1)}, u32[]{:S(2)}, u32[]{:S(2)}) %collective-permute-start.7) | collective-permute-done | bytes 131104 | tf_op jit(solution)/shard_map/ppermute | solution.py:18
  240.8 47.5 %all-gather.3 = f32[2048,32]{1,0:T(8,128)S(1)} all-gather(f32[32,32]{1,0:T(8,128)S(1)} %convolution_bitcast_fusion.2), channel_id=5, replica_groups=mesh['slab'=4,'xs'=64] {'xs'}, dimensions={0}, use_global_device_ids=true | all-gather | bytes 266240 | tf_op jit(solution)/shard_map/all_gather | solution.py:70
  288.5 2.9 custom-call.18
  292.8 2.4 custom-call.19
  297.4 2.4 collective-permute-start.10
  299.8 4.3 collective-permute-start.8
  304.1 1.9 collective-permute-start.9
  306.2 2.5 copy.18
  308.8 5.0 collective-permute-done.9
  313.7 2.5 fusion.43
  316.3 30.9 %collective-permute-done.10 = f32[32,16,1024]{2,0,1:T(8,128)S(1)} collective-permute-done((f32[32,16,1024]{2,0,1:T(8,128)S(1)}, f32[32,16,1024]{2,0,1:T(8,128)S(1)}, u32[]{:S(2)}, u32[]{:S(2)}) %collective-permute-start.10) | collective-permute-done | bytes 2097184 | tf_op jit(solution)/shard_map/ppermute | solution.py:27
  348.9 248.6 %all-reduce.5 = (f32[1,32,32]{2,1,0:T(8,128)}, f32[1,32,32]{2,1,0:T(8,128)}) all-reduce(f32[1,32,32]{2,1,0:T(8,128)S(1)} %fusion.43, f32[1,32,32]{2,1,0:T(8,128)S(1)} %convolution_bitcast_fusion), channel_id=1, replica_groups=mesh['slab'=4,'xs'=64] {'xs'}, use_global_device_ids=true, to_apply=%region_6.9 | all-reduce | flops 2048 | bytes 16384 | tf_op jit(solution)/shard_map/psum | solution.py:78
  (68 shorter events, 32.2 us)
Async XLA Ops:
  0.6 7.5 %copy-start = (s32[1,16,1024]{2,1,0:T(8,128)S(1)}, s32[1,16,1024]{2,1,0:T(8,128)}, u32[]{:S(2)}) copy-start(s32[1,16,1024]{2,1,0:T(8,128)} %param.5) | copy-start | bytes 196612
  2.2 6.4 %collective-permute-start = (f32[1,32,1,1024]{3,1,2,0:T(8,128)S(1)}, f32[1,32,1,1024]{3,1,2,0:T(8,128)S(1)}, u32[]{:S(2)}, u32[]{:S(2)}) collective-permute-start(f32[1,32,1,1024]{3,1,2,0:T(8,128)S(1)} %get-tuple-element.21), channel_id=1, source_target_pairs={{1,0},{2,1},{3,2},{4,3},{5,4},{6,5},{7,6},{8,7},{9,8},{10,9},{11,1... | collective-permute-start | bytes 393224 | tf_op jit(solution)/shard_map/ppermute | solution.py:19
  6.1 9.6 %collective-permute-start.1 = (f32[1,32,1,1024]{3,1,2,0:T(8,128)S(1)}, f32[1,32,1,1024]{3,1,2,0:T(8,128)S(1)}, u32[]{:S(2)}, u32[]{:S(2)}) collective-permute-start(f32[1,32,1,1024]{3,1,2,0:T(8,128)S(1)} %get-tuple-element.22), channel_id=1, source_target_pairs={{0,1},{1,2},{2,3},{3,4},{4,5},{5,6},{6,7},{7,8},{8,9},{9,10},{10,1... | collective-permute-start | bytes 393224 | tf_op jit(solution)/shard_map/ppermute | solution.py:18
  75.9 7.1 %collective-permute-start.2 = (f32[1,32,1,1024]{3,1,2,0:T(8,128)S(1)}, f32[1,32,1,1024]{3,1,2,0:T(8,128)S(1)}, u32[]{:S(2)}, u32[]{:S(2)}) collective-permute-start(f32[1,32,1,1024]{3,1,2,0:T(8,128)S(1)} %get-tuple-element.19), channel_id=1, source_target_pairs={{1,0},{2,1},{3,2},{4,3},{5,4},{6,5},{7,6},{8,7},{9,8},{10,9},{11,1... | collective-permute-start | bytes 393224 | tf_op jit(solution)/shard_map/ppermute | solution.py:19
  80.4 9.6 %collective-permute-start.3 = (f32[1,32,1,1024]{3,1,2,0:T(8,128)S(1)}, f32[1,32,1,1024]{3,1,2,0:T(8,128)S(1)}, u32[]{:S(2)}, u32[]{:S(2)}) collective-permute-start(f32[1,32,1,1024]{3,1,2,0:T(8,128)S(1)} %get-tuple-element.20), channel_id=1, source_target_pairs={{0,1},{1,2},{2,3},{3,4},{4,5},{5,6},{6,7},{7,8},{8,9},{9,10},{10,1... | collective-permute-start | bytes 393224 | tf_op jit(solution)/shard_map/ppermute | solution.py:18
  149.4 7.1 %collective-permute-start.4 = (f32[1,32,1,1024]{3,1,2,0:T(8,128)S(1)}, f32[1,32,1,1024]{3,1,2,0:T(8,128)S(1)}, u32[]{:S(2)}, u32[]{:S(2)}) collective-permute-start(f32[1,32,1,1024]{3,1,2,0:T(8,128)S(1)} %get-tuple-element.17), channel_id=1, source_target_pairs={{1,0},{2,1},{3,2},{4,3},{5,4},{6,5},{7,6},{8,7},{9,8},{10,9},{11,1... | collective-permute-start | bytes 393224 | tf_op jit(solution)/shard_map/ppermute | solution.py:19
  153.9 9.6 %collective-permute-start.5 = (f32[1,32,1,1024]{3,1,2,0:T(8,128)S(1)}, f32[1,32,1,1024]{3,1,2,0:T(8,128)S(1)}, u32[]{:S(2)}, u32[]{:S(2)}) collective-permute-start(f32[1,32,1,1024]{3,1,2,0:T(8,128)S(1)} %get-tuple-element.18), channel_id=1, source_target_pairs={{0,1},{1,2},{2,3},{3,4},{4,5},{5,6},{6,7},{7,8},{8,9},{9,10},{10,1... | collective-permute-start | bytes 393224 | tf_op jit(solution)/shard_map/ppermute | solution.py:18
  223.7 7.1 %collective-permute-start.6 = (f32[1,32,1,1024]{3,1,2,0:T(8,128)S(1)}, f32[1,32,1,1024]{3,1,2,0:T(8,128)S(1)}, u32[]{:S(2)}, u32[]{:S(2)}) collective-permute-start(f32[1,32,1,1024]{3,1,2,0:T(8,128)S(1)} %get-tuple-element.15), channel_id=1, source_target_pairs={{1,0},{2,1},{3,2},{4,3},{5,4},{6,5},{7,6},{8,7},{9,8},{10,9},{11,1... | collective-permute-start | bytes 393224 | tf_op jit(solution)/shard_map/ppermute | solution.py:19
  228.2 9.6 %collective-permute-start.7 = (f32[1,32,1,1024]{3,1,2,0:T(8,128)S(1)}, f32[1,32,1,1024]{3,1,2,0:T(8,128)S(1)}, u32[]{:S(2)}, u32[]{:S(2)}) collective-permute-start(f32[1,32,1,1024]{3,1,2,0:T(8,128)S(1)} %get-tuple-element.16), channel_id=1, source_target_pairs={{0,1},{1,2},{2,3},{3,4},{4,5},{5,6},{6,7},{7,8},{8,9},{9,10},{10,1... | collective-permute-start | bytes 393224 | tf_op jit(solution)/shard_map/ppermute | solution.py:18
  297.4 49.8 %collective-permute-start.10 = (f32[32,16,1024]{2,0,1:T(8,128)S(1)}, f32[32,16,1024]{2,0,1:T(8,128)S(1)}, u32[]{:S(2)}, u32[]{:S(2)}) collective-permute-start(f32[32,16,1024]{2,0,1:T(8,128)S(1)} %fusion.86), channel_id=1, source_target_pairs={{64,0},{128,64},{192,128},{65,1},{129,65},{193,129},{66,2},{130,66... | collective-permute-start | bytes 6291464 | tf_op jit(solution)/shard_map/ppermute | solution.py:27
  299.8 8.9 %collective-permute-start.8 = (f32[1,32,1,1024]{3,1,2,0:T(8,128)S(1)}, f32[1,32,1,1024]{3,1,2,0:T(8,128)S(1)}, u32[]{:S(2)}, u32[]{:S(2)}) collective-permute-start(f32[1,32,1,1024]{3,1,2,0:T(8,128)S(1)} %get-tuple-element.13), channel_id=1, source_target_pairs={{1,0},{2,1},{3,2},{4,3},{5,4},{6,5},{7,6},{8,7},{9,8},{10,9},{11,1... | collective-permute-start | bytes 393224 | tf_op jit(solution)/shard_map/ppermute | solution.py:19
  304.1 9.6 %collective-permute-start.9 = (f32[1,32,1,1024]{3,1,2,0:T(8,128)S(1)}, f32[1,32,1,1024]{3,1,2,0:T(8,128)S(1)}, u32[]{:S(2)}, u32[]{:S(2)}) collective-permute-start(f32[1,32,1,1024]{3,1,2,0:T(8,128)S(1)} %get-tuple-element.14), channel_id=1, source_target_pairs={{0,1},{1,2},{2,3},{3,4},{4,5},{5,6},{6,7},{7,8},{8,9},{9,10},{10,1... | collective-permute-start | bytes 393224 | tf_op jit(solution)/shard_map/ppermute | solution.py:18
